TPU v7x, 512 devices: a whole 4x8x8 slice. The times are simulated.
512 devices in a mesh: user: 32 (over z_lo, x, core), item: 16 (over z_hi, y).
Axes of the slice: x: 4, y: 8, z: 8 (z_hi: 2, z_lo: 4; z = z_hi * 4 + z_lo), core: 2. Of those that a mesh axis runs over, the one named last changes fastest.
Arguments:
- user_x: bfloat16 [131072, 512], P(('user', 'item')), may hold values from -120 to 120
- item_x: bfloat16 [131072, 512], P(('user', 'item')), may hold values from -6 to 6
- lin_proj: bfloat16 [131072, 256], P(('user', 'item')), may hold values from -0.015625 to 0.015625
- tile_lists: int32 [512, 16], P('user'), may hold values from 0 to 2, as said below
- w_q: bfloat16 [512, 512], replicated, may hold values from -0.25 to 0.25
- w_k: bfloat16 [512, 512], replicated, may hold values from -0.25 to 0.25
- w_v: bfloat16 [512, 512], replicated, may hold values from -0.25 to 0.25
- w_o: bfloat16 [512, 512], replicated, may hold values from -1 to 1
- cotangent: bfloat16 [131072, 512], P(('user', 'item')), may hold values from -6 to 6
Outputs:
- updated: bfloat16 [131072, 512], P(('user', 'item'))
- user_grad: bfloat16 [131072, 512], P(('user', 'item'))
- item_grad: bfloat16 [131072, 512], P(('user', 'item'))
Inputs may be any that keep to these rules, and one draw needn't show every extreme that they name: `tile_lists`: A value below 2 names a tile of item device j of block b's group; 2 means no tile from it. Every block takes at least one tile, and in every group of 16 blocks some block takes a tile from every item device of the group.
All inputs are finite; a program needn't handle non-finite values.
Results may differ from a plain program's by a relative error of at most 0.009.
Values may be sent and summed in bfloat16 or wider, within the bound.
A program may use at most 128 MiB of HBM per device.

v0:
```python
import jax
import jax.numpy as jnp
from jax import lax
from jax.sharding import PartitionSpec as P

HEADS = 8
TILE = 128


def head_major(matrix, head_count):
    row_count = matrix.shape[0]
    return matrix.reshape(row_count, head_count, -1).transpose(1, 0, 2)


def row_major(stacked):
    head_count, row_count, head_width = stacked.shape
    return stacked.transpose(1, 0, 2).reshape(row_count, head_count * head_width)


def per_device(user_x, item_x, lin_proj, tile_lists, w_q, w_k, w_v, w_o, cotangent):
    head_count = HEADS
    model_width = w_q.shape[0]
    tile_rows = TILE
    tiles_here = item_x.shape[0] // tile_rows
    owners = lax.axis_size("item")
    position = lax.axis_index("item")
    factor = (model_width // head_count) ** (-0.5)
    both_weights = jnp.concatenate([w_k, w_v], axis=1)
    item_kv = jnp.dot(item_x, both_weights, preferred_element_type=jnp.float32).astype(jnp.bfloat16)
    partial_kv = jnp.einsum("nr,nd->rd", lin_proj, item_kv, preferred_element_type=jnp.float32)
    lin_kv = lax.psum(partial_kv, ("user", "item")).astype(jnp.bfloat16)
    column = lax.dynamic_slice_in_dim(tile_lists, position, 1, 1)[:, 0]
    own_row = lax.dynamic_slice_in_dim(tile_lists, position, 1, 0)[0]
    chosen = (column[:, None] == jnp.arange(tiles_here)[None, :]).astype(jnp.bfloat16)
    live_slot = own_row < tiles_here
    tile_blocks = item_kv.reshape(tiles_here, tile_rows, 2 * model_width)
    outgoing = jnp.einsum(
        "ot,tkd->okd", chosen, tile_blocks, preferred_element_type=jnp.float32
    ).astype(jnp.bfloat16)
    arrived = lax.all_to_all(outgoing, "item", split_axis=0, concat_axis=0, tiled=True)
    flat_tiles = arrived.reshape(owners * tile_rows, 2 * model_width)
    keys_all = jnp.concatenate([flat_tiles[:, :model_width], lin_kv[:, :model_width]], axis=0)
    values_all = jnp.concatenate([flat_tiles[:, model_width:], lin_kv[:, model_width:]], axis=0)
    keep_key = jnp.concatenate(
        [jnp.repeat(live_slot, tile_rows), jnp.ones((lin_kv.shape[0],), dtype=bool)]
    )
    queries = jnp.dot(user_x, w_q, preferred_element_type=jnp.float32).astype(jnp.bfloat16)
    d_attended = jnp.einsum("ud,ed->ue", cotangent, w_o, preferred_element_type=jnp.float32).astype(
        jnp.bfloat16
    )

    def head_pass(operands):
        query_head, key_head, value_head, grad_head = operands
        scores = (
            jnp.einsum("ue,se->us", query_head, key_head, preferred_element_type=jnp.float32)
            * factor
        )
        scores = jnp.where(keep_key[None, :], scores, -1e30)
        row_max = jnp.max(scores, axis=-1, keepdims=True)
        expo = jnp.exp(scores - row_max)
        attn_probs = expo / jnp.sum(expo, axis=-1, keepdims=True)
        probs_b = attn_probs.astype(jnp.bfloat16)
        attended = jnp.einsum("us,se->ue", probs_b, value_head, preferred_element_type=jnp.float32)
        d_probs = jnp.einsum("ue,se->us", grad_head, value_head, preferred_element_type=jnp.float32)
        row_delta = jnp.sum(attn_probs * d_probs, axis=-1, keepdims=True)
        d_scores = (attn_probs * (d_probs - row_delta) * factor).astype(jnp.bfloat16)
        d_query = jnp.einsum("us,se->ue", d_scores, key_head, preferred_element_type=jnp.float32)
        d_key = jnp.einsum("us,ue->se", d_scores, query_head, preferred_element_type=jnp.float32)
        d_value = jnp.einsum("us,ue->se", probs_b, grad_head, preferred_element_type=jnp.float32)
        return (attended, d_query, d_key, d_value)

    operands = (
        head_major(queries, head_count),
        head_major(keys_all, head_count),
        head_major(values_all, head_count),
        head_major(d_attended, head_count),
    )
    attended, d_query, d_key, d_value = lax.map(head_pass, operands)
    attended_rows = row_major(attended).astype(jnp.bfloat16)
    updated = jnp.dot(attended_rows, w_o, preferred_element_type=jnp.float32).astype(jnp.bfloat16)
    query_rows = row_major(d_query).astype(jnp.bfloat16)
    user_grad = jnp.einsum("ud,ed->ue", query_rows, w_q, preferred_element_type=jnp.float32).astype(
        jnp.bfloat16
    )
    d_both = jnp.concatenate([row_major(d_key), row_major(d_value)], axis=1)
    tile_part = (
        d_both[: owners * tile_rows]
        .astype(jnp.bfloat16)
        .reshape(owners, tile_rows, 2 * model_width)
    )
    returned = lax.all_to_all(tile_part, "item", split_axis=0, concat_axis=0, tiled=True)
    grad_tiles = jnp.einsum(
        "ot,okd->tkd", chosen, returned, preferred_element_type=jnp.float32
    ).reshape(-1, 2 * model_width)
    lin_part = d_both[owners * tile_rows :]
    proj_float = lin_proj.astype(jnp.float32)
    back_weights = both_weights.astype(jnp.float32)
    lin_total = lax.psum(lin_part, ("user", "item"))
    kv_grad = grad_tiles + jnp.dot(proj_float, lin_total, precision=lax.Precision.HIGHEST)
    item_grad = jnp.einsum(
        "nd,ed->ne", kv_grad, back_weights, precision=lax.Precision.HIGHEST
    ).astype(jnp.bfloat16)
    return (updated, user_grad, item_grad)


def solution(mesh):
    return jax.shard_map(
        per_device,
        mesh=mesh,
        in_specs=(
            P(("user", "item"), None),
            P(("user", "item"), None),
            P(("user", "item"), None),
            P("user", None),
            P(),
            P(),
            P(),
            P(),
            P(("user", "item"), None),
        ),
        out_specs=(P(("user", "item"), None), P(("user", "item"), None), P(("user", "item"), None)),
        check_vma=False,
    )
```

profile of v0, /device:TPU:1, one launch (start us, length us, event | category | flops | bytes accessed | tf_op | source)
XLA Modules:
  0.0 763.0 jit_solution(17429336741048789214)
XLA Ops:
  7.2 1.2 constant_dynamic-update-slice_fusion.1
  10.4 1.6 convolution_convert_fusion.1
  11.9 1.6 convolution_convert_fusion
  13.6 4.3 copy.51
  17.8 16.4 %all-to-all-start = ((bf16[16,128,1024]{2,1,0:T(8,128)(2,1)}), bf16[16,128,1024]{2,1,0:T(8,128)(2,1)}, u32[]{:S(2)}, u32[]{:S(2)}) async-start(bf16[16,128,1024]{2,1,0:T(8,128)(2,1)} %copy.51), calls=%async_computation | async-start | bytes 8388608 | tf_op jit(solution)/shard_map/all_to_all | solution.py:40
  37.0 222.2 %all-reduce.5 = bf16[256,1024]{0,1:T(8,128)(2,1)S(1)} all-reduce(f32[256,1024]{0,1:T(8,128)S(1)} %convolution_bitcast_fusion.5), channel_id=1, replica_groups=mesh['user'=32,'item'=16] {'user','item'}, use_global_device_ids=true, to_apply=%region_0.0 | all-reduce | flops 262144 | bytes 1572864 | tf_op jit(solution)/shard_map/psum | solution.py:31
  260.3 2.5 fusion.45
  262.8 2.4 pad_maximum_fusion
  265.2 2.8 copy.53
  268.0 4.3 copy.55
  272.4 94.1 %while.16 = (s32[]{:T(128)}, bf16[8,256,64]{1,2,0:T(8,128)(2,1)}, bf16[8,256,64]{1,2,0:T(8,128)(2,1)}, f32[8,2304,64]{1,2,0:T(8,128)}, f32[8,2304,64]{1,2,0:T(8,...) while((s32[]{:T(128)}, bf16[8,256,64]{1,2,0:T(8,128)(2,1)}, ...), condition=%wide.region_5.6_spmd, body=%wide.region_1.5_spmd.sunk | while | flops 465370368 | bytes 25057396 | solution.py:78
  272.4 1.3 fusion.87
  274.2 2.2 fusion.89
  276.4 1.7 multiply_reduce_fusion.2
  278.9 1.1 fusion.90
  280.0 2.2 fusion.92
  282.2 1.9 fusion.91
  284.1 1.3 fusion.87
  285.9 2.2 fusion.89
  288.1 1.7 multiply_reduce_fusion.2
  291.7 2.2 fusion.92
  293.9 1.9 fusion.91
  295.9 1.4 fusion.87
  297.7 2.2 fusion.89
  299.9 1.7 multiply_reduce_fusion.2
  303.5 2.2 fusion.92
  305.7 1.9 fusion.91
  307.7 1.3 fusion.87
  309.5 2.2 fusion.89
  311.7 1.7 multiply_reduce_fusion.2
  315.3 2.2 fusion.92
  317.5 1.9 fusion.91
  319.4 1.3 fusion.87
  321.2 2.2 fusion.89
  323.4 1.7 multiply_reduce_fusion.2
  327.0 2.2 fusion.92
  329.2 1.9 fusion.91
  331.1 1.3 fusion.87
  332.9 2.2 fusion.89
  335.1 1.7 multiply_reduce_fusion.2
  338.7 2.2 fusion.92
  340.9 1.9 fusion.91
  342.8 1.3 fusion.87
  344.7 2.2 fusion.89
  346.9 1.7 multiply_reduce_fusion.2
  349.4 1.1 fusion.90
  350.5 2.2 fusion.92
  352.7 1.9 fusion.91
  354.6 1.3 fusion.87
  356.4 2.2 fusion.89
  358.7 1.7 multiply_reduce_fusion.2
  362.3 2.2 fusion.92
  364.5 1.9 fusion.91
  366.4 5.2 fusion.35
  371.6 6.4 copy.61
  378.0 7.7 %all-to-all-start.1 = ((bf16[16,128,1024]{2,1,0:T(8,128)(2,1)}), bf16[16,128,1024]{2,1,0:T(8,128)(2,1)}, u32[]{:S(2)}, u32[]{:S(2)}) async-start(bf16[16,128,1024]{2,1,0:T(8,128)(2,1)} %bitcast.147), calls=%async_computation.1 | async-start | bytes 8388608 | tf_op jit(solution)/shard_map/all_to_all | solution.py:91
  386.0 2.3 pad_maximum_fusion.2
  390.4 116.6 %all-to-all-done.1 = bf16[16,128,1024]{2,1,0:T(8,128)(2,1)} async-done(((bf16[16,128,1024]{2,1,0:T(8,128)(2,1)}), bf16[16,128,1024]{2,1,0:T(8,128)(2,1)}, u32[]{:S(2)}, u32[]{:S(2)}) %all-to-all-start.1) | async-done | bytes 4194336 | tf_op jit(solution)/shard_map/all_to_all | solution.py:91
  507.0 4.7 fusion.36
  511.7 1.3 copy.63
  513.1 1.6 copy.64
  514.7 237.0 %all-reduce.4.cloned.1.call-done = f32[256,1024]{0,1:T(8,128)} async-done(((f32[256,1024]{0,1:T(8,128)}), f32[256,1024]{0,1:T(8,128)}) %all-reduce.4.cloned.1.call-update) | async-done | bytes 1048592 | tf_op jit(solution)/shard_map/psum | solution.py:98
  751.7 1.8 fusion.38
  753.6 2.6 convolution_convert_fusion.2
  (62 shorter events, 24.6 us)
Async XLA Ops:
  7.2 28.3 %copy-start = (bf16[512,512]{1,0:T(8,128)(2,1)S(1)}, bf16[512,512]{1,0:T(8,128)(2,1)}, u32[]{:S(2)}) copy-start(bf16[512,512]{1,0:T(8,128)(2,1)} %param.18) | copy-start | bytes 1572868
  10.4 3.2 copy-start.1
  17.8 16.4 %copy-start.3 = (bf16[512,512]{1,0:T(8,128)(2,1)S(1)}, bf16[512,512]{1,0:T(8,128)(2,1)}, u32[]{:S(2)}) copy-start(bf16[512,512]{1,0:T(8,128)(2,1)} %param.15) | copy-start | bytes 1572868
  17.8 16.5 %copy-start.5 = (bf16[256,512]{1,0:T(8,128)(2,1)S(1)}, bf16[256,512]{1,0:T(8,128)(2,1)}, u32[]{:S(2)}) copy-start(bf16[256,512]{1,0:T(8,128)(2,1)} %param.11) | copy-start | bytes 786436
  17.8 17.6 %copy-start.6 = (bf16[256,512]{1,0:T(8,128)(2,1)S(1)}, bf16[256,512]{1,0:T(8,128)(2,1)}, u32[]{:S(2)}) copy-start(bf16[256,512]{1,0:T(8,128)(2,1)} %param.19) | copy-start | bytes 786436
  17.8 242.5 %all-to-all-start = ((bf16[16,128,1024]{2,1,0:T(8,128)(2,1)}), bf16[16,128,1024]{2,1,0:T(8,128)(2,1)}, u32[]{:S(2)}, u32[]{:S(2)}) async-start(bf16[16,128,1024]{2,1,0:T(8,128)(2,1)} %copy.51), calls=%async_computation | async-start | bytes 8388608 | tf_op jit(solution)/shard_map/all_to_all | solution.py:40
  34.2 2.4 copy-start.4
  378.0 129.0 %all-to-all-start.1 = ((bf16[16,128,1024]{2,1,0:T(8,128)(2,1)}), bf16[16,128,1024]{2,1,0:T(8,128)(2,1)}, u32[]{:S(2)}, u32[]{:S(2)}) async-start(bf16[16,128,1024]{2,1,0:T(8,128)(2,1)} %bitcast.147), calls=%async_computation.1 | async-start | bytes 8388608 | tf_op jit(solution)/shard_map/all_to_all | solution.py:91
  385.8 2.6 copy-start.8
  385.8 3.6 copy-start.7
  385.8 365.9 %all-reduce.4.cloned.1.call-start = ((), (), s32[]{:S(2)}) async-start(), calls=%async_computation.2 | async-start | bytes 2097152 | tf_op jit(solution)/shard_map/psum | solution.py:98
  513.1 240.5 %copy-start.2 = (bf16[512,1024]{1,0:T(8,128)(2,1)S(1)}, bf16[512,1024]{1,0:T(8,128)(2,1)}, u32[]{:S(2)}) copy-start(bf16[512,1024]{1,0:T(8,128)(2,1)} %copy-done.1) | copy-start | bytes 3145732
Sparse Core Ops, SparseCore 0:
  391.7 359.9 all-reduce.3
where the time goes:
time: 766 us; the launch traced here: 763 us
  waiting for transfers between devices  354 us (46%)
  blocking collectives  222 us (29%)
  matrix products  99.6 us (13%)
  local copies, waits for them, and re-layouts  28.6 us (4%)
  starting transfers between devices  24.3 us (3%)
  other arithmetic  20.3 us (3%)
  between operations  14.3 us (2%)
    psum x1, waiting for transfers between devices, per_device(): lin_total = lax.psum(lin_part, ('user', 'item'))  237 us
    psum x1, blocking collectives, per_device(): lin_kv = lax.psum(partial_kv, ('user', 'item')).astype(jnp.bfloat16)  222 us
    all_to_all x1, waiting for transfers between devices, per_device(): lax.all_to_all(tile_part, 'item', split_axis=0, concat_axis=0, tiled=True)  117 us
    dot_general x8, matrix products, head_pass(): jnp.einsum('us,se->ue', probs_b, value_head, preferred_element_type=jnp.f...  17.7 us
    dot_general x8, matrix products, head_pass(): jnp.einsum('us,ue->se', probs_b, grad_head, preferred_element_type=jnp.fl...  17.6 us
    all_to_all x1, starting transfers between devices, per_device(): lax.all_to_all(outgoing, 'item', split_axis=0, concat_axis=0, tiled=True)  16.4 us
    dot_general x8, matrix products, head_pass(): jnp.einsum('us,ue->se', d_scores, query_head, preferred_element_type=jnp....  15.4 us
  transfers between devices with their start and end apart: 3, of which 2 were waited for; matrix products, arithmetic and copies ran while one was open for 2% of the time, Pallas kernels for 0%

commit v1 on v0

v1 whole, which is shorter than its diff:
```python
import functools

import jax
import jax.numpy as jnp
from jax import lax
from jax.experimental import pallas as pl
from jax.experimental.pallas import tpu as pltpu
from jax.sharding import PartitionSpec as P

F32, BF16 = jnp.float32, jnp.bfloat16
HEADS, HEAD, WIDTH, TILE, RANK = 8, 64, 512, 128, 256
ROWS = 256
OWNERS = 16
KEYS = OWNERS * TILE + RANK
CHUNK = 256
CHUNKS = KEYS // CHUNK
VMEM_BYTES = 60 * 1024 * 1024
MESH = pl.DeviceIdType.MESH


def dot(a, b):
    return lax.dot_general(a, b, (((1,), (0,)), ((), ())), preferred_element_type=F32)


def dot_t(a, b):
    return lax.dot_general(a, b, (((1,), (1,)), ((), ())), preferred_element_type=F32)


def split(a):
    high = a.astype(BF16)
    return high, (a - high.astype(F32)).astype(BF16)


class Place:
    def __init__(self):
        self.user, self.item = lax.axis_index("user"), lax.axis_index("item")
        self.near = lax.rem(self.user, 8)
        self.z_lo = lax.div(self.user, 8)
        self.y = lax.rem(self.item, 8)
        self.z_hi = lax.div(self.item, 8)
        self.z = self.z_hi * 4 + self.z_lo
        self.member = (self.near, self.z, self.y)

    def peer(self, group, k):
        if group == 0:
            return (self.z_lo * 8 + k, self.item)
        if group == 1:
            return (lax.rem(k, 4) * 8 + self.near, lax.div(k, 4) * 8 + self.y)
        return (self.user, self.z_hi * 8 + k)

    def along_y(self, step):
        return lax.rem(self.y + step + 8, 8)

    def partner(self):
        return (self.user, lax.rem(self.item + 8, 16))


def greet(place):
    barrier = pltpu.get_barrier_semaphore()
    for group in range(3):
        for r in range(1, 8):
            k = lax.rem(place.member[group] + r, 8)
            pl.semaphore_signal(barrier, inc=1, device_id=place.peer(group, k), device_id_type=MESH)
    pl.semaphore_wait(barrier, 21)


class Total:
    scratch = [
        pltpu.VMEM((8, 32, WIDTH), F32),
        pltpu.VMEM((8, 8, 256), F32),
        pltpu.VMEM((8, 8, 256), F32),
        pltpu.VMEM((8, 256), F32),
        pltpu.VMEM((8, 8, 256), F32),
        pltpu.VMEM((8, 256), F32),
        pltpu.VMEM((8, 8, 256), F32),
        pltpu.VMEM((32, WIDTH), F32),
        pltpu.SemaphoreType.DMA((5, 8)),
        pltpu.SemaphoreType.DMA((5, 8)),
    ]

    def __init__(self, place, part, out, scratch):
        self.place, self.part, self.out = place, part, out
        (self.land1, self.s1, self.land2, self.s2, self.land3, self.s3, self.land4, self.s4) = scratch[:8]
        self.send_sem, self.recv_sem = scratch[8:]
        self.started = [[] for _ in range(5)]

    def start(self, phase, group, source, land):
        me = self.place.member[group]
        for r in range(1, 8):
            k = lax.rem(me + r, 8)
            copy = pltpu.make_async_remote_copy(
                src_ref=source(k),
                dst_ref=land.at[me],
                send_sem=self.send_sem.at[phase, r],
                recv_sem=self.recv_sem.at[phase, r],
                device_id=self.place.peer(group, k),
                device_id_type=MESH,
            )
            copy.start()
            self.started[phase].append(copy)

    def arrive(self, phase):
        for copy in self.started[phase]:
            copy.wait_recv()

    def step(self, phase):
        near, z, y = self.place.member
        if phase == 0:
            self.start(0, 0, lambda k: self.part.at[k], self.land1)
            self.land1[near] = self.part[near]
            return
        self.arrive(phase - 1)
        if phase == 1:
            total = self.land1[0]
            for k in range(1, 8):
                total = total + self.land1[k]
            for p in range(8):
                self.s1[p] = total[p // 2 * 8 : p // 2 * 8 + 8, p % 2 * 256 : p % 2 * 256 + 256]
            self.start(1, 1, lambda k: self.s1.at[k], self.land2)
            self.land2[z] = self.s1[z]
        elif phase == 2:
            total = self.land2[0]
            for k in range(1, 8):
                total = total + self.land2[k]
            self.s2[...] = total
            self.start(2, 2, lambda k: self.s2, self.land3)
            self.land3[y] = total
        elif phase == 3:
            total = self.land3[0]
            for k in range(1, 8):
                total = total + self.land3[k]
            self.s3[...] = total
            self.start(3, 1, lambda k: self.s3, self.land4)
            self.land4[z] = total
        elif phase == 4:
            for p in range(8):
                self.s4[p // 2 * 8 : p // 2 * 8 + 8, p % 2 * 256 : p % 2 * 256 + 256] = self.land4[p]
            self.start(4, 0, lambda k: self.s4, self.out)
            self.out[near] = self.s4[...]

    def finish(self):
        for copies in self.started:
            for copy in copies:
                copy.wait_send()


class Attention:
    scratch = [
        pltpu.VMEM((4, KEYS, 128), BF16),
        pltpu.VMEM((4, KEYS, 128), BF16),
        pltpu.VMEM((HEADS, HEAD, KEYS), BF16),
        pltpu.VMEM((HEADS, HEAD, CHUNK), BF16),
        pltpu.VMEM((HEADS, 128, ROWS), BF16),
        pltpu.VMEM((HEADS, 128, ROWS), BF16),
        pltpu.VMEM((4, 2 * ROWS, 128), BF16),
        pltpu.VMEM((4, 2 * ROWS, 128), BF16),
        pltpu.VMEM((HEADS, HEAD, ROWS), F32),
        pltpu.VMEM((HEADS, KEYS, ROWS), F32),
        pltpu.VMEM((CHUNK, 2 * WIDTH), F32),
        pltpu.VMEM((HEADS, HEAD, ROWS), F32),
        pltpu.VMEM((HEADS, HEAD, ROWS), F32),
        pltpu.VMEM((HEADS, 1, ROWS), F32),
        pltpu.VMEM((HEADS, 1, ROWS), F32),
        pltpu.VMEM((HEADS, 1, ROWS), F32),
        pltpu.VMEM((CHUNKS, HEADS, 1, ROWS), F32),
        pltpu.VMEM((WIDTH, WIDTH), BF16),
        pltpu.VMEM((WIDTH, WIDTH), BF16),
    ]

    def __init__(self, weights, scratch):
        self.wq, self.wk, self.wv, self.wo = weights
        (self.k_s, self.v_s, self.kt_s, self.vt_s, self.qt_m, self.at_m, self.q_m, self.a_m, self.at_s,
         self.e_s, self.dkv, self.o_t, self.dq_t, self.top, self.den, self.delta, self.tops,
         self.wk_t, self.wv_t) = scratch

    def prepare(self, user_ref, cot_ref):
        q = dot(user_ref[...], self.wq[...]).astype(BF16).astype(F32) * (HEAD**-0.5)
        a = dot_t(cot_ref[...], self.wo[...]).astype(BF16).astype(F32)
        qt, at = q.T, a.T
        self.at_s[...] = at.reshape(HEADS, HEAD, ROWS)
        low_lane = lax.broadcasted_iota(jnp.int32, (ROWS, 128), 1) < HEAD
        low_row = lax.broadcasted_iota(jnp.int32, (128, ROWS), 0) < HEAD
        for p in range(4):
            cut = slice(p * 128, p * 128 + 128)
            for hh in range(2):
                lane, row = (low_lane, low_row) if hh == 0 else (~low_lane, ~low_row)
                half = slice(hh * ROWS, hh * ROWS + ROWS)
                self.q_m[p, half] = jnp.where(lane, q[:, cut], 0.0).astype(BF16)
                self.a_m[p, half] = jnp.where(lane, a[:, cut], 0.0).astype(BF16)
                self.qt_m[2 * p + hh] = jnp.where(row, qt[cut], 0.0).astype(BF16)
                self.at_m[2 * p + hh] = jnp.where(row, at[cut], 0.0).astype(BF16)
        self.wk_t[...] = self.wk[...].astype(F32).T.astype(BF16)
        self.wv_t[...] = self.wv[...].astype(F32).T.astype(BF16)
        self.top[...] = jnp.full(self.top.shape, -1e30, F32)
        self.den[...] = jnp.zeros(self.den.shape, F32)
        self.o_t[...] = jnp.zeros(self.o_t.shape, F32)
        self.dq_t[...] = jnp.zeros(self.dq_t.shape, F32)

    def forward(self, c, pieces, live):
        at_rows = slice(c * CHUNK, c * CHUNK + CHUNK)
        k = sum(dot(piece, self.wk[...]) for piece in pieces).astype(BF16)
        v = sum(dot(piece, self.wv[...]) for piece in pieces).astype(BF16)
        for p in range(4):
            self.k_s[p, at_rows] = k[:, p * 128 : p * 128 + 128]
            self.v_s[p, at_rows] = v[:, p * 128 : p * 128 + 128]
        kt = sum(dot_t(self.wk_t[...], piece) for piece in pieces).astype(BF16)
        vt = sum(dot_t(self.wv_t[...], piece) for piece in pieces).astype(BF16)
        self.kt_s[:, :, at_rows] = kt.reshape(HEADS, HEAD, CHUNK)
        self.vt_s[...] = vt.reshape(HEADS, HEAD, CHUNK)

        def pair(p, carry):
            for hh in range(2):
                h = 2 * p + hh
                s = dot(self.k_s[p, at_rows], self.qt_m[h])
                if live is not None:
                    s = jnp.concatenate(
                        [jnp.where(live[0], s[:TILE], -1e30), jnp.where(live[1], s[TILE:], -1e30)], axis=0
                    )
                before = self.top[h]
                top = jnp.maximum(before, jnp.max(s, axis=0, keepdims=True))
                e = jnp.exp(s - top)
                scale = jnp.exp(before - top)
                self.top[h] = top
                self.tops[c, h] = top
                self.e_s[h, at_rows] = e
                self.den[h] = self.den[h] * scale + jnp.sum(e, axis=0, keepdims=True)
                self.o_t[h] = self.o_t[h] * scale + dot(self.vt_s[h], e.astype(BF16))
            return carry

        lax.fori_loop(0, 4, pair, 0)

    def settle(self):
        for h in range(HEADS):
            inverse = 1.0 / self.den[h]
            o = self.o_t[h] * inverse
            self.o_t[h] = o
            self.den[h] = inverse
            self.delta[h] = jnp.sum(o * self.at_s[h], axis=0, keepdims=True)

    def backward(self, c):
        at_rows = slice(c * CHUNK, c * CHUNK + CHUNK)

        def pair(p, carry):
            ds, pb = [], []
            for hh in range(2):
                h = 2 * p + hh
                dp = dot(self.v_s[p, at_rows], self.at_m[h])
                prob = self.e_s[h, at_rows] * (jnp.exp(self.tops[c, h] - self.top[h]) * self.den[h])
                pb.append(prob.astype(BF16))
                ds.append((prob * (dp - self.delta[h])).astype(BF16))
                self.dq_t[h] = self.dq_t[h] + dot(self.kt_s[h, :, at_rows], ds[hh])
            self.dkv[:, pl.ds(pl.multiple_of(p * 128, 128), 128)] = dot(
                jnp.concatenate(ds, axis=1), self.q_m[p]
            )
            self.dkv[:, pl.ds(pl.multiple_of(WIDTH + p * 128, 128), 128)] = dot(
                jnp.concatenate(pb, axis=1), self.a_m[p]
            )
            return carry

        lax.fori_loop(0, 4, pair, 0)
        if c < CHUNKS - 1:
            pieces = (self.dkv[...].astype(BF16),)
        else:
            pieces = split(self.dkv[...])
        return sum(
            dot_t(piece[:, :WIDTH], self.wk[...]) + dot_t(piece[:, WIDTH:], self.wv[...]) for piece in pieces
        )

    def updated(self):
        attended = self.o_t[...].reshape(WIDTH, ROWS).T.astype(BF16)
        return dot(attended, self.wo[...]).astype(BF16)

    def user_grad(self):
        d_query = (self.dq_t[...] * (HEAD**-0.5)).reshape(WIDTH, ROWS).T.astype(BF16)
        return dot_t(d_query, self.wq[...]).astype(BF16)


RING = [
    pltpu.SemaphoreType.DMA,
    pltpu.SemaphoreType.DMA,
    pltpu.SemaphoreType.DMA((2, 2, 5)),
    pltpu.SemaphoreType.DMA((2, 2, 5)),
]


class Gather:
    def __init__(self, place, x_ref, all_ref, sems):
        self.place, self.x, self.all = place, x_ref, all_ref
        self.zs, self.zr, self.send_sem, self.recv_sem = sems
        self.ring = {}

    def column(self, chain):
        return (self.place.z_hi if chain == 0 else 1 - self.place.z_hi) * 8

    def start_across(self):
        self.across = pltpu.make_async_remote_copy(
            src_ref=self.x, dst_ref=self.all.at[self.place.item], send_sem=self.zs, recv_sem=self.zr,
            device_id=self.place.partner(), device_id_type=MESH,
        )
        self.across.start()

    def send(self, chain, way, d):
        step = 1 if way == 0 else -1
        index = self.column(chain) + self.place.along_y(-step * (d - 1))
        source = self.x if (chain == 0 and d == 1) else self.all.at[index]
        target = self.all.at[index]
        if d == 4:
            source, target = source.at[pl.ds(way * TILE, TILE)], target.at[pl.ds(way * TILE, TILE)]
        copy = pltpu.make_async_remote_copy(
            src_ref=source, dst_ref=target,
            send_sem=self.send_sem.at[chain, way, d], recv_sem=self.recv_sem.at[chain, way, d],
            device_id=(self.place.user, self.place.z_hi * 8 + self.place.along_y(step)), device_id_type=MESH,
        )
        copy.start()
        self.ring[chain, way, d] = copy

    def forward(self, chain, d):
        for way in range(2):
            self.ring[chain, way, d].wait_recv()
            if d < 4:
                self.send(chain, way, d + 1)

    def finish(self):
        self.across.wait_send()
        for copy in self.ring.values():
            copy.wait_send()


class Scatter:
    scratch = [
        pltpu.VMEM((2, 2, 4, ROWS, WIDTH), BF16),
        pltpu.VMEM((2, 2, 4, ROWS, WIDTH), BF16),
        pltpu.VMEM((ROWS, WIDTH), BF16),
        pltpu.VMEM((ROWS, WIDTH), BF16),
    ] + RING

    def __init__(self, place, listed, scratch):
        self.place, self.listed = place, listed
        (self.leave, self.land, self.z_buf, self.z_land, self.zs, self.zr, self.send_sem, self.recv_sem) = scratch
        self.ring = {}

    def send(self, chain, way, d, own):
        step = 1 if way == 0 else -1
        buf, target = self.leave.at[chain, way, d - 1], self.land.at[chain, way, d - 1]
        if d < 4:
            self.ring[chain, way, d + 1].wait_recv()
        for tile in range(2):
            if d == 4 and tile != way:
                continue
            rows = slice(tile * TILE, tile * TILE + TILE)
            value = own(tile)
            if d < 3 or (d == 3 and tile == way):
                value = value + self.land[chain, way, d, rows].astype(F32)
            self.leave[chain, way, d - 1, rows] = value.astype(BF16)
        if d == 4:
            buf, target = buf.at[pl.ds(way * TILE, TILE)], target.at[pl.ds(way * TILE, TILE)]
        copy = pltpu.make_async_remote_copy(
            src_ref=buf, dst_ref=target,
            send_sem=self.send_sem.at[chain, way, d], recv_sem=self.recv_sem.at[chain, way, d],
            device_id=(self.place.user, self.place.z_hi * 8 + self.place.along_y(step)), device_id_type=MESH,
        )
        copy.start()
        self.ring[chain, way, d] = copy

    def total(self, chain, own, tile):
        rows = slice(tile * TILE, tile * TILE + TILE)
        value = own(tile)
        return value + self.land[chain, 0, 0, rows].astype(F32) + self.land[chain, 1, 0, rows].astype(F32)

    def arrive(self, chain):
        for way in range(2):
            self.ring[chain, way, 1].wait_recv()

    def start_across(self, own):
        for tile in range(2):
            self.z_buf[tile * TILE : tile * TILE + TILE] = self.total(1, own, tile).astype(BF16)
        self.across = pltpu.make_async_remote_copy(
            src_ref=self.z_buf, dst_ref=self.z_land, send_sem=self.zs, recv_sem=self.zr,
            device_id=self.place.partner(), device_id_type=MESH,
        )
        self.across.start()

    def finish(self):
        self.across.wait_send()
        for copy in self.ring.values():
            copy.wait_send()


def take(scratch, count):
    taken = scratch[:count]
    del scratch[:count]
    return taken


def kernel(
    row_ref, user_ref, x_ref, proj_ref, wq_ref, wk_ref, wv_ref, wo_ref, cot_ref,
    upd_ref, ug_ref, out_ref, all_x, part, lin_sum, lin_total, grads, own_part, *scratch
):
    scratch = list(scratch)
    place = Place()
    gather = Gather(place, x_ref, all_x, take(scratch, 4))
    scatter = Scatter(place, row_ref, take(scratch, len(Scatter.scratch)))
    lin = Total(place, part, lin_sum, take(scratch, len(Total.scratch)))
    d_lin = Total(place, own_part, lin_total, take(scratch, len(Total.scratch)))
    attention = Attention((wq_ref, wk_ref, wv_ref, wo_ref), scratch)

    greet(place)
    gather.start_across()
    for way in range(2):
        gather.send(0, way, 1)
    total = lax.dot_general(
        proj_ref[...], x_ref[...], (((0,), (0,)), ((), ())), preferred_element_type=F32
    )
    for k in range(8):
        part[k] = total[k * 32 : k * 32 + 32]
    lin.step(0)
    attention.prepare(user_ref, cot_ref)
    lin.step(1)
    gather.forward(0, 1)
    lin.step(2)
    gather.across.wait_recv()
    for way in range(2):
        gather.send(1, way, 1)
    lin.step(3)

    def listed(chain, dy):
        return row_ref[gather.column(chain) + place.along_y(dy)]

    def chunk_forward(dy):
        rows, live = [], []
        for chain in range(2):
            tile = listed(chain, dy)
            block = x_ref if (chain == 0 and dy == 0) else all_x.at[gather.column(chain) + place.along_y(dy)]
            rows.append(jnp.where(tile == 1, block[TILE:], block[:TILE]))
            live.append(tile < 2)
        attention.forward(dy, (jnp.concatenate(rows, axis=0),), live)

    chunk_forward(0)
    gather.forward(0, 2)
    lin.step(4)
    gather.forward(1, 1)
    chunk_forward(7)
    gather.forward(0, 3)
    chunk_forward(1)
    gather.forward(1, 2)
    chunk_forward(6)
    chunk_forward(2)
    gather.forward(1, 3)
    chunk_forward(5)
    chunk_forward(3)
    lin.arrive(4)
    attention.forward(8, split(lin_sum[...].reshape(RANK, WIDTH)), None)
    gather.forward(0, 4)
    gather.forward(1, 4)
    chunk_forward(4)
    attention.settle()

    g = attention.backward(8)
    for k in range(8):
        own_part[k] = g[k * 32 : k * 32 + 32]
    d_lin.step(0)

    def chunk_backward(dy):
        grads[...] = attention.backward(dy)

    def own(chain, dy):
        def term(tile):
            return jnp.where(listed(chain, dy) == tile, grads[chain * TILE : chain * TILE + TILE], 0.0)

        return term

    chunk_backward(4)
    for chain in (1, 0):
        for way in range(2):
            scatter.send(chain, way, 4, own(chain, 4))
    d_lin.step(1)
    for d in (3, 2, 1):
        for way in range(2):
            dy = d if way == 0 else 8 - d
            chunk_backward(dy)
            for chain in (1, 0):
                scatter.send(chain, way, d, own(chain, dy))
        d_lin.step(5 - d)
    chunk_backward(0)
    upd_ref[...] = attention.updated()
    ug_ref[...] = attention.user_grad()
    scatter.arrive(1)
    scatter.start_across(own(1, 0))
    d_lin.arrive(4)
    back = jnp.zeros((ROWS, WIDTH), F32)
    for piece in split(lin_total[...].reshape(RANK, WIDTH)):
        back = back + dot(proj_ref[...], piece)
    scatter.arrive(0)
    scatter.across.wait_recv()
    for tile in range(2):
        rows = slice(tile * TILE, tile * TILE + TILE)
        value = back[rows] + scatter.total(0, own(0, 0), tile) + scatter.z_land[rows].astype(F32)
        out_ref[rows] = value.astype(BF16)
    lin.finish()
    d_lin.finish()
    gather.finish()
    scatter.finish()


def in_vmem(count):
    return [pl.BlockSpec(memory_space=pltpu.VMEM)] * count


def per_device(user_x, item_x, lin_proj, tile_lists, w_q, w_k, w_v, w_o, cotangent):
    position = lax.axis_index("item")
    own_row = lax.dynamic_slice_in_dim(tile_lists, position, 1, 0)[0]
    shape = jax.ShapeDtypeStruct
    sums = pltpu.VMEM((8, 32, WIDTH), F32)
    return pl.pallas_call(
        kernel,
        out_shape=[shape((ROWS, WIDTH), BF16)] * 3,
        in_specs=[pl.BlockSpec(memory_space=pltpu.SMEM)] + in_vmem(8),
        out_specs=in_vmem(3),
        scratch_shapes=[
            pltpu.VMEM((OWNERS, ROWS, WIDTH), BF16),
            sums, sums, sums,
            pltpu.VMEM((CHUNK, WIDTH), F32),
            sums,
        ] + RING + Scatter.scratch + Total.scratch + Total.scratch + Attention.scratch,
        compiler_params=pltpu.CompilerParams(
            collective_id=0, has_side_effects=True, vmem_limit_bytes=VMEM_BYTES
        ),
        name="attend_and_exchange",
    )(own_row, user_x, item_x, lin_proj, w_q, w_k, w_v, w_o, cotangent)


def solution(mesh):
    rows = P(("user", "item"), None)
    return jax.shard_map(
        per_device,
        mesh=mesh,
        in_specs=(rows, rows, rows, P("user", None), P(), P(), P(), P(), rows),
        out_specs=(rows, rows, rows),
        check_vma=False,
    )
```

time: 766 us -> 149 us (0.19)
  waiting for transfers between devices: 354 us -> 0 us
  blocking collectives: 222 us -> 0 us
  Pallas kernels: 0 us -> 144 us
  matrix products: 99.6 us -> 0 us
  starting transfers between devices: 24.3 us -> 0 us
  local copies, waits for them, and re-layouts: 28.6 us -> 4.67 us
  other arithmetic: 20.3 us -> 0 us
  between operations: 14.3 us -> 0.66 us
    psum x1 -> x0, waiting for transfers between devices: 237 us -> none  [per_device(): lin_total = lax.psum(lin_part, ('user', 'item'))]
    psum x1 -> x0, blocking collectives: 222 us -> none  [per_device(): lin_kv = lax.psum(partial_kv, ('user', 'item')).astype(jnp.bfloat16)]
    pallas_call x0 -> x1, Pallas kernels: none -> 144 us  [per_device(): pl.pallas_call(kernel, out_shape=[shape((ROWS, WIDTH), BF16)] * 3, in_spe...]
    all_to_all x2 -> x0, waiting for transfers between devices: 117 us -> none  [the longest x1 117 us: per_device(): lax.all_to_all(tile_part, 'item', split_axis=0, concat_axis=0, tiled=True)]
    dot_general x58 -> x0, matrix products: 99.6 us -> none  [the longest x8 17.7 us: head_pass(): jnp.einsum('us,se->ue', probs_b, value_head, preferred_element_type=jnp.f...]
    all_to_all x2 -> x0, starting transfers between devices: 24.1 us -> none  [the longest x1 16.4 us: per_device(): lax.all_to_all(outgoing, 'item', split_axis=0, concat_axis=0, tiled=True)]
    slice x5 -> x0, local copies, waits for them, and re-layouts: 9.24 us -> none  [the longest x1 6.43 us: per_device(): d_both[:owners * tile_rows].astype(jnp.bfloat16)]
    concatenate x4 -> x0, local copies, waits for them, and re-layouts: 8.27 us -> none  [the longest x1 4.32 us: per_device(): jnp.concatenate([flat_tiles[:, model_width:], lin_kv[:, model_width:]], a...]
  transfers between devices with their start and end apart: 3 -> 0, of which waited for: 2 -> 0; matrix products, arithmetic and copies ran while one was open for 2% -> 0% of each run, Pallas kernels for 0% -> 0%
where the time goes in v1:
time: 149 us
  Pallas kernels  144 us (97%)
  local copies, waits for them, and re-layouts  4.67 us (3%)
    pallas_call x1, Pallas kernels, per_device(): pl.pallas_call(kernel, out_shape=[shape((ROWS, WIDTH), BF16)] * 3, in_spe...  144 us
    unnamed x9, local copies, waits for them, and re-layouts  4.15 us

profile of v1, /device:TPU:1, one launch (start us, length us, event | category | flops | bytes accessed | tf_op | source)
XLA Modules:
  0.0 149.0 jit_solution(3779125013063209529)
XLA Ops:
  0.6 0.0 copy-start
  0.6 0.7 copy-done
  1.3 0.5 dynamic-slice_bitcast_fusion.row_ref
  1.8 143.7 %attend_and_exchange.1 = (bf16[256,512]{1,0:T(8,128)(2,1)}, bf16[256,512]{1,0:T(8,128)(2,1)}, bf16[256,512]{1,0:T(8,128)(2,1)}) custom-call(s32[16]{0:T(128)} %dynamic-slice_bitcast_fusion.row_ref, bf16[256,512]{1,0:T(8,128)(2,1)} %user_ref.1, bf16[256,512]{1,0:T(8,128)(2,1)} %x_ref.1, bf16[256,256]{1,0:T(8,128)(2,1)} %proj_ref.1, bf16[512,512]{1,0:T(8,128)(2,1)} %wq_ref.1, ...), custom_call_target="tpu_custom_call" | custom-call | tf_op jit(solution)/shard_map/attend_and_exchange/pallas_call | solution.py:514
  145.6 0.0 copy-start.2
  145.6 1.7 %copy.15 = bf16[256,512]{1,0:T(8,128)(2,1)} copy(bf16[256,512]{1,0:T(8,128)(2,1)} %get-tuple-element.6) | data formatting | bytes 524288
  147.3 0.0 copy-done.2
  147.3 0.0 copy-start.1
  147.3 0.7 copy.16
  148.0 0.3 copy-done.1
  148.3 0.7 copy.17
Async XLA Ops:
  0.6 0.7 copy-start
  145.6 1.7 %copy-start.2 = (bf16[256,512]{1,0:T(8,128)(2,1)S(1)}, bf16[256,512]{1,0:T(8,128)(2,1)}, u32[]{:S(2)}) copy-start(bf16[256,512]{1,0:T(8,128)(2,1)} %get-tuple-element.7) | copy-start | bytes 786436
  147.3 1.0 copy-start.1

commit v2 on v1

--- a/solution.py
+++ b/solution.py
@@ -275,115 +275,215 @@
         return dot_t(d_query, self.wq[...]).astype(BF16)
 
 
-RING = [
-    pltpu.SemaphoreType.DMA,
-    pltpu.SemaphoreType.DMA,
-    pltpu.SemaphoreType.DMA((2, 2, 5)),
-    pltpu.SemaphoreType.DMA((2, 2, 5)),
-]
-
-
-class Gather:
-    def __init__(self, place, x_ref, all_ref, sems):
-        self.place, self.x, self.all = place, x_ref, all_ref
-        self.zs, self.zr, self.send_sem, self.recv_sem = sems
-        self.ring = {}
+def ring_peer(place, way, hops=1):
+    return place.z_hi * 8 + place.along_y(hops if way == 0 else -hops)
+
+
+class Ring:
+    semaphores = [
+        pltpu.SemaphoreType.DMA((2, 2, 8)),
+        pltpu.SemaphoreType.DMA((2, 2, 8)),
+        pltpu.SemaphoreType.DMA((2,)),
+        pltpu.SemaphoreType.DMA((2,)),
+    ]
+
+    def __init__(self, place, sems):
+        self.place = place
+        self.send_sem, self.recv_sem, self.zs, self.zr = sems
+        self.copies, self.across = {}, {}
 
     def column(self, chain):
         return (self.place.z_hi if chain == 0 else 1 - self.place.z_hi) * 8
 
-    def start_across(self):
-        self.across = pltpu.make_async_remote_copy(
-            src_ref=self.x, dst_ref=self.all.at[self.place.item], send_sem=self.zs, recv_sem=self.zr,
+    def push(self, chain, way, number, source, target):
+        copy = pltpu.make_async_remote_copy(
+            src_ref=source, dst_ref=target,
+            send_sem=self.send_sem.at[chain, way, number], recv_sem=self.recv_sem.at[chain, way, number],
+            device_id=(self.place.user, ring_peer(self.place, way)), device_id_type=MESH,
+        )
+        copy.start()
+        self.copies[chain, way, number] = copy
+
+    def wait(self, chain, way, number):
+        self.copies[chain, way, number].wait_recv()
+
+    def cross(self, tile, source, target):
+        copy = pltpu.make_async_remote_copy(
+            src_ref=source, dst_ref=target, send_sem=self.zs.at[tile], recv_sem=self.zr.at[tile],
             device_id=self.place.partner(), device_id_type=MESH,
         )
-        self.across.start()
-
-    def send(self, chain, way, d):
-        step = 1 if way == 0 else -1
-        index = self.column(chain) + self.place.along_y(-step * (d - 1))
-        source = self.x if (chain == 0 and d == 1) else self.all.at[index]
-        target = self.all.at[index]
-        if d == 4:
-            source, target = source.at[pl.ds(way * TILE, TILE)], target.at[pl.ds(way * TILE, TILE)]
-        copy = pltpu.make_async_remote_copy(
-            src_ref=source, dst_ref=target,
-            send_sem=self.send_sem.at[chain, way, d], recv_sem=self.recv_sem.at[chain, way, d],
-            device_id=(self.place.user, self.place.z_hi * 8 + self.place.along_y(step)), device_id_type=MESH,
-        )
         copy.start()
-        self.ring[chain, way, d] = copy
-
-    def forward(self, chain, d):
+        self.across[tile] = copy
+
+    def finish(self):
+        for copy in list(self.across.values()) + list(self.copies.values()):
+            copy.wait_send()
+
+
+def tile_rows(tile):
+    return pl.ds(tile * TILE, TILE)
+
+
+class Gather(Ring):
+    scratch = [
+        pltpu.VMEM((2, 2, TILE, WIDTH), BF16),
+        pltpu.VMEM((2, 2, TILE // 2, WIDTH), BF16),
+        pltpu.VMEM((2, 2, TILE, WIDTH), BF16),
+        pltpu.VMEM((2, 2, TILE // 2, WIDTH), BF16),
+        pltpu.VMEM((2, 2, TILE // 2, WIDTH), BF16),
+    ] + Ring.semaphores
+
+    def __init__(self, place, lists, x_ref, all_ref, scratch):
+        self.lists, self.x, self.all = lists, x_ref, all_ref
+        self.out3, self.out4, self.in3, self.via3, self.in4 = scratch[:5]
+        super().__init__(place, scratch[5:])
+
+    def source(self, chain, way, hops):
+        return self.column(chain) + self.place.along_y(-hops if way == 0 else hops)
+
+    def block(self, chain, index, own):
+        return self.x if own and chain == 0 else self.all.at[index]
+
+    def cross_tile(self, tile):
+        self.cross(tile, self.x.at[tile_rows(tile)], self.all.at[self.place.item, tile_rows(tile)])
+
+    def first(self, chain, tile):
+        index = self.source(chain, 0, 0)
         for way in range(2):
-            self.ring[chain, way, d].wait_recv()
-            if d < 4:
-                self.send(chain, way, d + 1)
-
-    def finish(self):
-        self.across.wait_send()
-        for copy in self.ring.values():
-            copy.wait_send()
-
-
-class Scatter:
+            source = self.block(chain, index, True).at[tile_rows(tile)]
+            self.push(chain, way, tile, source, self.all.at[index, tile_rows(tile)])
+
+    def second(self, chain):
+        for tile in range(2):
+            for way in range(2):
+                self.wait(chain, way, tile)
+                part = self.all.at[self.source(chain, way, 1), tile_rows(tile)]
+                self.push(chain, way, 2 + tile, part, part)
+
+    def third(self, chain):
+        for way in range(2):
+            index = self.source(chain, way, 2)
+            for tile in range(2):
+                self.wait(chain, way, 2 + tile)
+            far = self.lists[ring_peer(self.place, way, 2), index] == 1
+            low = way * (TILE // 2)
+            self.out4[chain, way] = jnp.where(
+                far,
+                self.all[index, TILE + low : TILE + low + TILE // 2],
+                self.all[index, low : low + TILE // 2],
+            )
+            self.push(chain, way, 4, self.out4.at[chain, way], self.via3.at[chain, way])
+            near = self.lists[ring_peer(self.place, way, 1), index] == 1
+            self.out3[chain, way] = jnp.where(near, self.all[index, TILE:], self.all[index, :TILE])
+            self.push(chain, way, 5, self.out3.at[chain, way], self.in3.at[chain, way])
+
+    def fourth(self, chain):
+        for way in range(2):
+            self.wait(chain, way, 4)
+            self.push(chain, way, 6, self.via3.at[chain, way], self.in4.at[chain, way])
+
+    def tiles(self, chain, e):
+        found, live = [], []
+        for way in ((1, 0) if e else (None, 4)):
+            hops = 4 if way == 4 else e
+            index = self.source(chain, 0 if way in (None, 4) else way, hops)
+            tile = self.lists[self.place.item, index]
+            live.append(tile < 2)
+            if way == 4:
+                for way in range(2):
+                    self.wait(chain, way, 6)
+                    found.append(self.in4[chain, way])
+            elif e == 3:
+                self.wait(chain, way, 5)
+                found.append(self.in3[chain, way])
+            else:
+                block = self.block(chain, index, e == 0)
+                found.append(jnp.where(tile == 1, block[TILE:], block[:TILE]))
+        return jnp.concatenate(found, axis=0), live
+
+
+class Scatter(Ring):
     scratch = [
-        pltpu.VMEM((2, 2, 4, ROWS, WIDTH), BF16),
-        pltpu.VMEM((2, 2, 4, ROWS, WIDTH), BF16),
-        pltpu.VMEM((ROWS, WIDTH), BF16),
-        pltpu.VMEM((ROWS, WIDTH), BF16),
-    ] + RING
-
-    def __init__(self, place, listed, scratch):
-        self.place, self.listed = place, listed
-        (self.leave, self.land, self.z_buf, self.z_land, self.zs, self.zr, self.send_sem, self.recv_sem) = scratch
-        self.ring = {}
-
-    def send(self, chain, way, d, own):
-        step = 1 if way == 0 else -1
-        buf, target = self.leave.at[chain, way, d - 1], self.land.at[chain, way, d - 1]
-        if d < 4:
-            self.ring[chain, way, d + 1].wait_recv()
+        pltpu.VMEM((2, 2, TILE // 2, WIDTH), BF16),
+        pltpu.VMEM((2, 2, TILE // 2, WIDTH), BF16),
+        pltpu.VMEM((2, 2, TILE // 2, WIDTH), BF16),
+        pltpu.VMEM((2, 2, TILE, WIDTH), BF16),
+        pltpu.VMEM((2, 2, TILE, WIDTH), BF16),
+        pltpu.VMEM((2, 2, 2, TILE, WIDTH), BF16),
+        pltpu.VMEM((2, 2, 2, TILE, WIDTH), BF16),
+        pltpu.VMEM((2, 2, 2, TILE, WIDTH), BF16),
+        pltpu.VMEM((2, 2, 2, TILE, WIDTH), BF16),
+        pltpu.VMEM((2, TILE, WIDTH), BF16),
+        pltpu.VMEM((2, TILE, WIDTH), BF16),
+        pltpu.VMEM((8, CHUNK, WIDTH), F32),
+    ] + Ring.semaphores
+
+    def __init__(self, place, lists, scratch):
+        self.lists = lists
+        (self.out4, self.via3, self.in4, self.out3, self.in3, self.out2, self.in2, self.out1, self.in1,
+         self.z_out, self.z_in, self.grads) = scratch[:12]
+        super().__init__(place, scratch[12:])
+
+    def owner(self, chain, way, hops):
+        return self.column(chain) + self.place.along_y(hops if way == 0 else -hops)
+
+    def own(self, chain, way, e):
+        return self.grads[chain * 4 + e, tile_rows(0 if way == 0 else 1)]
+
+    def lists_here(self, index, tile):
+        return self.lists[self.place.item, index] == tile
+
+    def send4(self, chain):
+        for way in range(2):
+            low = TILE + way * (TILE // 2)
+            self.out4[chain, way] = self.grads[chain * 4, low : low + TILE // 2].astype(BF16)
+            self.push(chain, way, 0, self.out4.at[chain, way], self.via3.at[chain, way])
+
+    def send3(self, chain):
+        for way in range(2):
+            self.out3[chain, way] = self.own(chain, way, 3).astype(BF16)
+            self.wait(chain, way, 0)
+            self.push(chain, way, 1, self.via3.at[chain, way], self.in4.at[chain, way])
+            self.push(chain, way, 2, self.out3.at[chain, way], self.in3.at[chain, way])
+
+    def send2(self, chain):
+        for way in range(2):
+            index = self.owner(chain, way, 2)
+            one, two = ring_peer(self.place, way, -1), ring_peer(self.place, way, -2)
+            self.wait(chain, way, 1)
+            self.wait(chain, way, 2)
+            half = slice(way * (TILE // 2), way * (TILE // 2) + TILE // 2)
+            other = slice((1 - way) * (TILE // 2), (1 - way) * (TILE // 2) + TILE // 2)
+            for tile in range(2):
+                value = jnp.where(self.lists_here(index, tile), self.own(chain, way, 2), 0.0)
+                value = value + jnp.where(
+                    self.lists[one, index] == tile, self.in3[chain, way].astype(F32), 0.0
+                )
+                far = jnp.where(self.lists[two, index] == tile, self.in4[chain, way].astype(F32), 0.0)
+                self.out2[chain, way, tile, half] = (value[half] + far).astype(BF16)
+                self.out2[chain, way, tile, other] = value[other].astype(BF16)
+                self.push(chain, way, 3 + tile, self.out2.at[chain, way, tile], self.in2.at[chain, way, tile])
+
+    def send1(self, chain):
         for tile in range(2):
-            if d == 4 and tile != way:
-                continue
-            rows = slice(tile * TILE, tile * TILE + TILE)
-            value = own(tile)
-            if d < 3 or (d == 3 and tile == way):
-                value = value + self.land[chain, way, d, rows].astype(F32)
-            self.leave[chain, way, d - 1, rows] = value.astype(BF16)
-        if d == 4:
-            buf, target = buf.at[pl.ds(way * TILE, TILE)], target.at[pl.ds(way * TILE, TILE)]
-        copy = pltpu.make_async_remote_copy(
-            src_ref=buf, dst_ref=target,
-            send_sem=self.send_sem.at[chain, way, d], recv_sem=self.recv_sem.at[chain, way, d],
-            device_id=(self.place.user, self.place.z_hi * 8 + self.place.along_y(step)), device_id_type=MESH,
-        )
-        copy.start()
-        self.ring[chain, way, d] = copy
-
-    def total(self, chain, own, tile):
-        rows = slice(tile * TILE, tile * TILE + TILE)
-        value = own(tile)
-        return value + self.land[chain, 0, 0, rows].astype(F32) + self.land[chain, 1, 0, rows].astype(F32)
-
-    def arrive(self, chain):
+            for way in range(2):
+                index = self.owner(chain, way, 1)
+                self.wait(chain, way, 3 + tile)
+                value = jnp.where(self.lists_here(index, tile), self.own(chain, way, 1), 0.0)
+                value = value + self.in2[chain, way, tile].astype(F32)
+                self.out1[chain, way, tile] = value.astype(BF16)
+                self.push(chain, way, 5 + tile, self.out1.at[chain, way, tile], self.in1.at[chain, way, tile])
+
+    def total(self, chain, tile):
         for way in range(2):
-            self.ring[chain, way, 1].wait_recv()
-
-    def start_across(self, own):
+            self.wait(chain, way, 5 + tile)
+        value = jnp.where(self.lists_here(self.owner(chain, 0, 0), tile), self.own(chain, 0, 0), 0.0)
+        return value + self.in1[chain, 0, tile].astype(F32) + self.in1[chain, 1, tile].astype(F32)
+
+    def send_across(self):
         for tile in range(2):
-            self.z_buf[tile * TILE : tile * TILE + TILE] = self.total(1, own, tile).astype(BF16)
-        self.across = pltpu.make_async_remote_copy(
-            src_ref=self.z_buf, dst_ref=self.z_land, send_sem=self.zs, recv_sem=self.zr,
-            device_id=self.place.partner(), device_id_type=MESH,
-        )
-        self.across.start()
-
-    def finish(self):
-        self.across.wait_send()
-        for copy in self.ring.values():
-            copy.wait_send()
+            self.z_out[tile] = self.total(1, tile).astype(BF16)
+            self.cross(tile, self.z_out.at[tile], self.z_in.at[tile])
 
 
 def take(scratch, count):
@@ -393,21 +493,28 @@
 
 
 def kernel(
-    row_ref, user_ref, x_ref, proj_ref, wq_ref, wk_ref, wv_ref, wo_ref, cot_ref,
-    upd_ref, ug_ref, out_ref, all_x, part, lin_sum, lin_total, grads, own_part, *scratch
+    lists_ref, user_ref, x_ref, proj_ref, wq_ref, wk_ref, wv_ref, wo_ref, cot_ref,
+    upd_ref, ug_ref, out_ref, all_x, part, lin_sum, lin_total, own_part, *scratch
 ):
     scratch = list(scratch)
     place = Place()
-    gather = Gather(place, x_ref, all_x, take(scratch, 4))
-    scatter = Scatter(place, row_ref, take(scratch, len(Scatter.scratch)))
+    gather = Gather(place, lists_ref, x_ref, all_x, take(scratch, len(Gather.scratch)))
+    scatter = Scatter(place, lists_ref, take(scratch, len(Scatter.scratch)))
     lin = Total(place, part, lin_sum, take(scratch, len(Total.scratch)))
     d_lin = Total(place, own_part, lin_total, take(scratch, len(Total.scratch)))
     attention = Attention((wq_ref, wk_ref, wv_ref, wo_ref), scratch)
 
+    def chunk_forward(chain, e):
+        rows, live = gather.tiles(chain, e)
+        attention.forward(chain * 4 + e, (rows,), live)
+
+    def chunk_backward(chain, e):
+        scatter.grads[chain * 4 + e] = attention.backward(chain * 4 + e)
+
     greet(place)
-    gather.start_across()
-    for way in range(2):
-        gather.send(0, way, 1)
+    for tile in range(2):
+        gather.first(0, tile)
+        gather.cross_tile(tile)
     total = lax.dot_general(
         proj_ref[...], x_ref[...], (((0,), (0,)), ((), ())), preferred_element_type=F32
     )
@@ -415,87 +522,66 @@
         part[k] = total[k * 32 : k * 32 + 32]
     lin.step(0)
     attention.prepare(user_ref, cot_ref)
+    gather.second(0)
+    chunk_forward(0, 1)
     lin.step(1)
-    gather.forward(0, 1)
+    gather.third(0)
+    for tile in range(2):
+        gather.across[tile].wait_recv()
+        gather.first(1, tile)
+    chunk_forward(0, 2)
     lin.step(2)
-    gather.across.wait_recv()
-    for way in range(2):
-        gather.send(1, way, 1)
+    gather.fourth(0)
+    chunk_forward(0, 3)
     lin.step(3)
-
-    def listed(chain, dy):
-        return row_ref[gather.column(chain) + place.along_y(dy)]
-
-    def chunk_forward(dy):
-        rows, live = [], []
-        for chain in range(2):
-            tile = listed(chain, dy)
-            block = x_ref if (chain == 0 and dy == 0) else all_x.at[gather.column(chain) + place.along_y(dy)]
-            rows.append(jnp.where(tile == 1, block[TILE:], block[:TILE]))
-            live.append(tile < 2)
-        attention.forward(dy, (jnp.concatenate(rows, axis=0),), live)
-
-    chunk_forward(0)
-    gather.forward(0, 2)
+    gather.second(1)
+    chunk_forward(0, 0)
+    chunk_forward(1, 1)
     lin.step(4)
-    gather.forward(1, 1)
-    chunk_forward(7)
-    gather.forward(0, 3)
-    chunk_forward(1)
-    gather.forward(1, 2)
-    chunk_forward(6)
-    chunk_forward(2)
-    gather.forward(1, 3)
-    chunk_forward(5)
-    chunk_forward(3)
+    gather.third(1)
+    chunk_forward(1, 2)
+    gather.fourth(1)
     lin.arrive(4)
     attention.forward(8, split(lin_sum[...].reshape(RANK, WIDTH)), None)
-    gather.forward(0, 4)
-    gather.forward(1, 4)
-    chunk_forward(4)
+    chunk_forward(1, 3)
+    chunk_forward(1, 0)
     attention.settle()
 
+    chunk_backward(1, 0)
+    scatter.send4(1)
+    chunk_backward(1, 3)
+    scatter.send3(1)
+    chunk_backward(0, 0)
+    scatter.send4(0)
     g = attention.backward(8)
     for k in range(8):
         own_part[k] = g[k * 32 : k * 32 + 32]
     d_lin.step(0)
-
-    def chunk_backward(dy):
-        grads[...] = attention.backward(dy)
-
-    def own(chain, dy):
-        def term(tile):
-            return jnp.where(listed(chain, dy) == tile, grads[chain * TILE : chain * TILE + TILE], 0.0)
-
-        return term
-
-    chunk_backward(4)
-    for chain in (1, 0):
-        for way in range(2):
-            scatter.send(chain, way, 4, own(chain, 4))
+    chunk_backward(1, 2)
+    scatter.send2(1)
+    chunk_backward(0, 3)
+    scatter.send3(0)
     d_lin.step(1)
-    for d in (3, 2, 1):
-        for way in range(2):
-            dy = d if way == 0 else 8 - d
-            chunk_backward(dy)
-            for chain in (1, 0):
-                scatter.send(chain, way, d, own(chain, dy))
-        d_lin.step(5 - d)
-    chunk_backward(0)
+    chunk_backward(1, 1)
+    scatter.send1(1)
+    chunk_backward(0, 2)
+    scatter.send2(0)
+    d_lin.step(2)
+    chunk_backward(0, 1)
+    scatter.send_across()
+    d_lin.step(3)
+    scatter.send1(0)
     upd_ref[...] = attention.updated()
     ug_ref[...] = attention.user_grad()
-    scatter.arrive(1)
-    scatter.start_across(own(1, 0))
+    d_lin.step(4)
     d_lin.arrive(4)
     back = jnp.zeros((ROWS, WIDTH), F32)
     for piece in split(lin_total[...].reshape(RANK, WIDTH)):
         back = back + dot(proj_ref[...], piece)
-    scatter.arrive(0)
-    scatter.across.wait_recv()
     for tile in range(2):
-        rows = slice(tile * TILE, tile * TILE + TILE)
-        value = back[rows] + scatter.total(0, own(0, 0), tile) + scatter.z_land[rows].astype(F32)
-        out_ref[rows] = value.astype(BF16)
+        value = back[tile * TILE : tile * TILE + TILE] + scatter.total(0, tile)
+        scatter.across[tile].wait_recv()
+        out_ref[tile * TILE : tile * TILE + TILE] = (value + scatter.z_in[tile].astype(F32)).astype(BF16)
     lin.finish()
     d_lin.finish()
     gather.finish()
@@ -507,8 +593,6 @@
 
 
 def per_device(user_x, item_x, lin_proj, tile_lists, w_q, w_k, w_v, w_o, cotangent):
-    position = lax.axis_index("item")
-    own_row = lax.dynamic_slice_in_dim(tile_lists, position, 1, 0)[0]
     shape = jax.ShapeDtypeStruct
     sums = pltpu.VMEM((8, 32, WIDTH), F32)
     return pl.pallas_call(
@@ -518,15 +602,13 @@
         out_specs=in_vmem(3),
         scratch_shapes=[
             pltpu.VMEM((OWNERS, ROWS, WIDTH), BF16),
-            sums, sums, sums,
-            pltpu.VMEM((CHUNK, WIDTH), F32),
-            sums,
-        ] + RING + Scatter.scratch + Total.scratch + Total.scratch + Attention.scratch,
+            sums, sums, sums, sums,
+        ] + Gather.scratch + Scatter.scratch + Total.scratch + Total.scratch + Attention.scratch,
         compiler_params=pltpu.CompilerParams(
             collective_id=0, has_side_effects=True, vmem_limit_bytes=VMEM_BYTES
         ),
         name="attend_and_exchange",
-    )(own_row, user_x, item_x, lin_proj, w_q, w_k, w_v, w_o, cotangent)
+    )(tile_lists, user_x, item_x, lin_proj, w_q, w_k, w_v, w_o, cotangent)
 
 
 def solution(mesh):

time: 149 us -> 135 us (0.906)
  Pallas kernels: 144 us -> 131 us
    pallas_call x1, Pallas kernels: 144 us -> 131 us  [per_device(): pl.pallas_call(kernel, out_shape=[shape((ROWS, WIDTH), BF16)] * 3, in_spe...]
    unnamed x9 -> x7, local copies, waits for them, and re-layouts: 4.15 us -> 3.46 us
where the time goes in v2:
time: 135 us
  Pallas kernels  131 us (97%)
  local copies, waits for them, and re-layouts  3.46 us (3%)
    pallas_call x1, Pallas kernels, per_device(): pl.pallas_call(kernel, out_shape=[shape((ROWS, WIDTH), BF16)] * 3, in_spe...  131 us
    unnamed x7, local copies, waits for them, and re-layouts  3.46 us

profile of v2, /device:TPU:1, one launch (start us, length us, event | category | flops | bytes accessed | tf_op | source)
XLA Modules:
  0.0 134.9 jit_solution(18208442666219691204)
XLA Ops:
  0.6 130.8 %attend_and_exchange.1 = (bf16[256,512]{1,0:T(8,128)(2,1)}, bf16[256,512]{1,0:T(8,128)(2,1)}, bf16[256,512]{1,0:T(8,128)(2,1)}) custom-call(s32[16,16]{1,0:T(8,128)} %lists_ref.1, bf16[256,512]{1,0:T(8,128)(2,1)} %user_ref.1, bf16[256,512]{1,0:T(8,128)(2,1)} %x_ref.1, bf16[256,256]{1,0:T(8,128)(2,1)} %proj_ref.1, bf16[512,512]{1,0:T(8,128)(2,1)} %wq_ref.1, ...), custom_call_target="tpu_custom_call" | custom-call | tf_op jit(solution)/shard_map/attend_and_exchange/pallas_call | solution.py:598
  131.4 0.0 copy-start.1
  131.4 1.7 %copy.15 = bf16[256,512]{1,0:T(8,128)(2,1)} copy(bf16[256,512]{1,0:T(8,128)(2,1)} %get-tuple-element.6) | data formatting | bytes 524288
  133.2 0.0 copy-done.1
  133.2 0.0 copy-start
  133.2 0.7 copy.16
  133.9 0.3 copy-done
  134.2 0.7 copy.17
Async XLA Ops:
  131.4 1.7 %copy-start.1 = (bf16[256,512]{1,0:T(8,128)(2,1)S(1)}, bf16[256,512]{1,0:T(8,128)(2,1)}, u32[]{:S(2)}) copy-start(bf16[256,512]{1,0:T(8,128)(2,1)} %get-tuple-element.7) | copy-start | bytes 786436
  133.2 1.0 copy-start
